TPU v7x, 256 devices: a whole 4x4x8 slice. The times are simulated.
256 devices in a mesh: expert: 32 (over y, z), dp: 8 (over x, core).
Axes of the slice: x: 4, y: 4, z: 8, core: 2. Of those that a mesh axis runs over, the one named last changes fastest.
Arguments:
- tokens: bfloat16 [32768, 7168], P(('expert', 'dp')), may hold values from -16 to 16
- norm_gain: float32 [7168], replicated, may hold values from 0.1 to 1.9
- routing: int32 [32768, 1], P(('expert', 'dp')), may hold values from 0 to 31; in each aligned block of 128 rows (0 to 127, 128 to 255, ...) at most 6 rows name the same one
- route_gate: float32 [32768], P(('expert', 'dp')), may hold values from 0.2 to 2
- gate_weight: bfloat16 [32, 7168, 1024], P('expert', 'dp'), may hold values from -0.0625 to 0.0625
- up_weight: bfloat16 [32, 7168, 1024], P('expert', 'dp'), may hold values from -0.0625 to 0.0625
- down_weight: bfloat16 [32, 1024, 7168], P('expert', None, 'dp'), may hold values from -0.1875 to 0.1875
- final_gain: float32 [7168], replicated, may hold values from 0.1 to 1.9
- unembed: bfloat16 [65536, 7168], P(('expert', 'dp')), may hold values from -16 to 16
- targets: int32 [512], P(('expert', 'dp')), may hold values from 0 to 65535
Outputs:
- layer_out: bfloat16 [32768, 7168], P(('expert', 'dp'))
- log_probs: float32 [512], replicated
Inputs may be any that keep to these rules, and one draw needn't show every extreme that they name: `routing`: in each block of 128 consecutive tokens (the tokens of one device) no expert is named by more than 6 tokens.
All inputs are finite; a program needn't handle non-finite values.
Results may differ from a plain program's by a relative error of at most 0.023.
Values may be sent and summed in bfloat16 or wider, within the bound.
A program may use at most 128 MiB of HBM per device.

v0:
```python
import jax
import jax.numpy as jnp
from jax import lax
from jax.sharding import PartitionSpec as P

LP_DEV = 2


EPSILON = 1e-06


def rms_scale(values, scale_gain):
    wide = values.astype(jnp.float32)
    mean_sq = jnp.mean(wide * wide, axis=-1, keepdims=True)
    return (wide * lax.rsqrt(mean_sq + EPSILON) * scale_gain).astype(jnp.bfloat16)


def activate(summed, units):
    return (jax.nn.silu(summed[:, :units]) * summed[:, units:]).astype(jnp.bfloat16)


def local(
    tokens,
    norm_gain,
    routing,
    route_gate,
    gate_weight,
    up_weight,
    down_weight,
    final_gain,
    unembed,
    targets,
):
    expert_count = lax.axis_size("expert")
    dp_count = lax.axis_size("dp")
    tok_rows = tokens.shape[0]
    width = tokens.shape[1]
    capacity = max(2, 3 * tok_rows // (2 * expert_count))
    units = up_weight.shape[2]
    normed = rms_scale(tokens, norm_gain)
    expert = routing[:, 0]
    onehot = (expert[:, None] == jnp.arange(expert_count, dtype=jnp.int32)[None, :]).astype(
        jnp.int32
    )
    slot_rank = jnp.sum((jnp.cumsum(onehot, axis=0) - onehot) * onehot, axis=1)
    slot_index = expert * capacity + slot_rank
    placer = (
        slot_index[:, None] == jnp.arange(expert_count * capacity, dtype=jnp.int32)[None, :]
    ).astype(jnp.bfloat16)
    outgoing = jnp.einsum("ts,td->sd", placer, normed, preferred_element_type=jnp.float32).astype(
        jnp.bfloat16
    )
    outgoing = outgoing.reshape(expert_count, capacity, width)
    arrived = lax.all_to_all(
        lax.all_to_all(outgoing, "expert", split_axis=0, concat_axis=0, tiled=True),
        "dp",
        split_axis=2,
        concat_axis=0,
        tiled=True,
    )
    dispatched = arrived.reshape(dp_count * expert_count * capacity, -1)
    gate_local = gate_weight[0]
    up_local = up_weight[0]
    down_local = down_weight[0]
    summed = lax.psum_scatter(
        jnp.concatenate(
            [
                jnp.dot(dispatched, gate_local, preferred_element_type=jnp.float32),
                jnp.dot(dispatched, up_local, preferred_element_type=jnp.float32),
            ],
            axis=1,
        ).astype(jnp.bfloat16),
        "dp",
        scatter_dimension=0,
        tiled=True,
    ).astype(jnp.float32)
    hidden = activate(summed, units)
    projected = jnp.dot(
        lax.all_gather(hidden, "dp", axis=0, tiled=True),
        down_local,
        preferred_element_type=jnp.float32,
    ).astype(jnp.bfloat16)
    returning = projected.reshape(dp_count * expert_count, capacity, -1)
    returned = lax.all_to_all(
        lax.all_to_all(returning, "dp", split_axis=0, concat_axis=2, tiled=True),
        "expert",
        split_axis=0,
        concat_axis=0,
        tiled=True,
    )
    picked_rows = jnp.dot(placer, returned.reshape(-1, width), preferred_element_type=jnp.float32)
    layer_out = (tokens.astype(jnp.float32) + route_gate[:, None] * picked_rows).astype(
        jnp.bfloat16
    )
    final_local = rms_scale(layer_out[:LP_DEV], final_gain)
    final_all, target_all = (
        lax.all_gather(final_local, ("expert", "dp"), axis=0, tiled=True),
        lax.all_gather(targets, ("expert", "dp"), axis=0, tiled=True),
    )
    logits = lax.dot_general(
        final_all, unembed, (((1,), (1,)), ((), ())), preferred_element_type=jnp.float32
    )
    vocab_rows = unembed.shape[0]
    vocab_start = (lax.axis_index("expert") * dp_count + lax.axis_index("dp")) * vocab_rows
    local_ids = target_all - vocab_start
    matches = local_ids[:, None] == jnp.arange(vocab_rows, dtype=jnp.int32)[None, :]
    picked = jnp.sum(jnp.where(matches, logits, 0.0), axis=1)
    row_top = jnp.max(logits, axis=1)
    row_top = lax.pmax(row_top, ("expert", "dp"))
    row_total = jnp.sum(jnp.exp(logits - row_top[:, None]), axis=1)
    row_total, picked = lax.psum((row_total, picked), ("expert", "dp"))
    log_probs = picked - (row_top + jnp.log(row_total))
    return (layer_out, log_probs)


def solution(mesh):
    placed = (
        P(("expert", "dp"), None),
        P(),
        P(("expert", "dp"), None),
        P(("expert", "dp")),
        P("expert", "dp", None),
        P("expert", "dp", None),
        P("expert", None, "dp"),
        P(),
        P(("expert", "dp"), None),
        P(("expert", "dp")),
    )
    return jax.shard_map(
        local,
        mesh=mesh,
        in_specs=placed,
        out_specs=(P(("expert", "dp"), None), P()),
        check_vma=False,
    )
```

profile of v0, /device:TPU:1, one launch (start us, length us, event | category | flops | bytes accessed | tf_op | source)
XLA Modules:
  0.0 779.4 jit_solution(2163897558303220074)
XLA Ops:
  7.2 0.0 copy-start
  7.2 0.0 reduce-scatter.4.cloned.1.call-start
  7.2 0.9 fusion.14
  8.1 0.2 reduce_window_sum.11
  8.3 0.8 select_reduce_fusion.1
  9.1 0.7 fusion.19
  9.8 1.9 fusion.2
  11.7 4.1 convolution_convert_fusion
  15.8 4.6 reshape.39
  20.4 93.8 %all_to_all.43 = bf16[32,6,7168]{2,1,0:T(8,128)(2,1)} all-to-all(bf16[32,6,7168]{2,1,0:T(8,128)(2,1)} %reshape.39), channel_id=1, replica_groups=mesh['expert'=32,'dp'=8] {'expert'}, dimensions={0} | all-to-all | bytes 5505024 | tf_op jit(solution)/shard_map/all_to_all | solution.py:55
  114.2 15.6 %copy.22 = bf16[32,6,7168]{0,1,2:T(8,128)(2,1)} copy(bf16[32,6,7168]{2,1,0:T(8,128)(2,1)} %all_to_all.43) | data formatting | bytes 5505024 | tf_op jit(solution)/shard_map/all_to_all | solution.py:55
  129.8 14.0 %reshape.49 = bf16[8,2,86016]{2,1,0:T(2,128)(2,1)} reshape(bf16[7168,6,32]{2,1,0:T(8,128)(2,1)} %bitcast.39) | data formatting | bytes 5505024
  143.8 41.8 %all_to_all.44 = bf16[8,2,86016]{2,1,0:T(2,128)(2,1)} all-to-all(bf16[8,2,86016]{2,1,0:T(2,128)(2,1)} %reshape.49), channel_id=1, replica_groups=mesh['expert'=32,'dp'=8] {'dp'}, dimensions={0} | all-to-all | bytes 5505024 | tf_op jit(solution)/shard_map/all_to_all | solution.py:54
  185.6 12.1 %reshape.50 = bf16[7168,6,32]{2,1,0:T(8,128)(2,1)} reshape(bf16[8,2,86016]{2,1,0:T(2,128)(2,1)} %all_to_all.44) | data formatting | bytes 5505024
  197.7 15.4 %copy.24 = bf16[8,32,6,896]{3,2,1,0:T(8,128)(2,1)} copy(bf16[8,32,6,896]{1,2,3,0:T(8,128)(2,1)} %bitcast.40) | data formatting | bytes 5505024 | tf_op jit(solution)/shard_map/all_to_all | solution.py:54
  213.1 5.6 reshape.40
  218.7 0.0 copy-done
  218.7 0.0 copy-start.3
  218.7 0.0 copy-start.7
  218.7 5.7 convolution_convert_fusion.1
  224.3 0.0 copy-done.3
  224.3 0.0 copy-done.7
  224.4 3.8 convolution_convert_fusion.2
  228.2 3.1 pad_maximum_fusion
  231.2 8.7 %copy.30 = bf16[1536,2048]{1,0:T(8,128)(2,1)} copy(bf16[1536,2048]{0,1:T(8,128)(2,1)} %pad_maximum_fusion) | data formatting | bytes 12582912
  239.9 0.0 reduce-scatter.4.cloned.1.call-update
  239.9 0.2 all-gather.4.cloned.1.call-start
  240.2 39.8 %reduce-scatter.4.cloned.1.call-done = bf16[192,2048]{1,0:T(8,128)(2,1)} async-done(((bf16[1536,2048]{1,0:T(8,128)(2,1)}), bf16[192,2048]{1,0:T(8,128)(2,1)}) %reduce-scatter.4.cloned.1.call-update) | async-done | bytes 786448
  280.0 1.4 copy.31
  281.4 0.2 convert_element_type.37
  281.6 0.3 fusion.11
  281.9 0.9 copy.25
  282.8 0.0 all-gather.4.cloned.1.call-update
  282.9 0.0 all-gather.6.cloned.1.call-start
  282.9 31.1 %all-gather.4.cloned.1.call-done = bf16[1536,1024]{1,0:T(8,128)(2,1)} async-done(((bf16[192,1024]{1,0:T(8,128)(2,1)}), bf16[1536,1024]{1,0:T(8,128)(2,1)}) %all-gather.4.cloned.1.call-update) | async-done | bytes 3145744 | tf_op jit(solution)/shard_map/all_gather | solution.py:79
  314.0 7.4 convolution_convert_fusion.3
  321.4 5.5 reshape.41
  327.0 47.4 %all_to_all.45 = bf16[256,6,896]{2,1,0:T(8,128)(2,1)S(1)} all-to-all(bf16[256,6,896]{2,1,0:T(8,128)(2,1)} %reshape.41), channel_id=1, replica_groups=mesh['expert'=32,'dp'=8] {'dp'}, dimensions={0} | all-to-all | bytes 5505024 | tf_op jit(solution)/shard_map/all_to_all | solution.py:85
  374.4 3.1 copy.33
  377.5 5.4 all_to_all.37
  382.9 3.3 copy.27
  386.2 90.6 %all_to_all.46 = bf16[32,6,7168]{2,1,0:T(8,128)(2,1)} all-to-all(bf16[32,6,7168]{2,1,0:T(8,128)(2,1)S(1)} %copy.27), channel_id=1, replica_groups=mesh['expert'=32,'dp'=8] {'expert'}, dimensions={0} | all-to-all | bytes 5505024 | tf_op jit(solution)/shard_map/all_to_all | solution.py:84
  476.8 4.8 reshape.42
  481.5 0.0 copy-done.2
  481.5 0.0 copy-done.6
  481.5 0.0 copy-start.8
  481.5 2.7 fusion.1
  484.2 0.0 copy-start.4
  484.2 0.2 fusion.15
  484.4 1.0 copy-done.4
  485.5 0.0 copy-done.5
  485.5 0.7 fusion.18
  486.2 0.0 all-gather.6.cloned.1.call-update
  486.2 0.0 copy-done.8
  486.2 0.2 dynamic-update-slice
  486.5 77.6 %all-reduce = s32[512]{0:T(512)S(1)} all-reduce(s32[512]{0:T(512)S(1)} %dynamic-update-slice), channel_id=1, replica_groups=mesh['expert'=32,'dp'=8] {'expert','dp'}, use_global_device_ids=true, to_apply=%add | all-reduce | flops 512 | bytes 4096
  564.1 38.3 %all-gather.6.cloned.1.call-done = bf16[256,2,7168]{2,1,0:T(2,128)(2,1)} async-done(((bf16[1,2,7168]{2,1,0:T(2,128)(2,1)}), bf16[256,2,7168]{2,1,0:T(2,128)(2,1)}) %all-gather.6.cloned.1.call-update) | async-done | bytes 7340048 | tf_op jit(solution)/shard_map/all_gather | solution.py:97
  602.4 15.4 %reshape.46 = bf16[512,7168]{1,0:T(8,128)(2,1)} reshape(bf16[256,2,7168]{2,1,0:T(2,128)(2,1)} %all-gather.6.cloned.1.call-done) | data formatting | bytes 14680064
  617.8 6.4 fusion.20
  624.2 75.3 %pmax.7 = f32[512]{0:T(512)S(1)} all-reduce(f32[512]{0:T(512)S(1)} %get-tuple-element.6), channel_id=1, replica_groups=mesh['expert'=32,'dp'=8] {'expert','dp'}, use_global_device_ids=true, to_apply=%region_8.9 | all-reduce | flops 512 | bytes 4096 | tf_op jit(solution)/shard_map/pmax | solution.py:109
  699.5 0.1 exponential_reduce_fusion
  699.6 72.7 %all-reduce.1 = (f32[512]{0:T(512)S(1)}, f32[512]{0:T(512)S(1)}) all-reduce(f32[512]{0:T(512)S(1)} %get-tuple-element.3, f32[512]{0:T(512)S(1)} %get-tuple-element.2), channel_id=1, replica_groups=mesh['expert'=32,'dp'=8] {'expert','dp'}, use_global_device_ids=true, to_apply=%region_6.7 | all-reduce | flops 1024 | bytes 8192 | tf_op jit(solution)/shard_map/psum | solution.py:111
  772.3 0.6 add_subtract_fusion
  772.9 0.0 copy-done.1
  (8 shorter events, 0.0 us)
Async XLA Ops:
  7.2 211.5 %copy-start = (bf16[1,896,1024]{2,1,0:T(8,128)(2,1)S(1)}, bf16[1,896,1024]{2,1,0:T(8,128)(2,1)}, u32[]{:S(2)}) copy-start(bf16[1,896,1024]{2,1,0:T(8,128)(2,1)} %param.15) | copy-start | bytes 5505028
  7.2 272.8 %reduce-scatter.4.cloned.1.call-start = ((), (), s32[]{:S(2)}) async-start(), calls=%async_computation.7 | async-start | bytes 7077888
  218.7 5.7 copy-start.3
  218.7 5.7 copy-start.7
  239.9 74.1 %all-gather.4.cloned.1.call-start = ((), (), s32[]{:S(2)}) async-start(), calls=%async_computation.5 | async-start | bytes 3538944 | tf_op jit(solution)/shard_map/all_gather | solution.py:79
  282.9 319.5 %all-gather.6.cloned.1.call-start = ((), (), s32[]{:S(2)}) async-start(), calls=%async_computation.6 | async-start | bytes 7368704 | tf_op jit(solution)/shard_map/all_gather | solution.py:97
  476.8 4.8 copy-start.2
  476.8 4.8 copy-start.6
  481.5 3.9 copy-start.5
  481.5 4.7 copy-start.8
  484.2 1.2 copy-start.4
  617.8 155.1 %copy-start.1 = (bf16[1,896,1024]{2,1,0:T(8,128)(2,1)S(1)}, bf16[1,896,1024]{2,1,0:T(8,128)(2,1)}, u32[]{:S(2)}) copy-start(bf16[1,896,1024]{2,1,0:T(8,128)(2,1)} %param.15) | copy-start | bytes 5505028
Sparse Core Ops, SparseCore 0:
  240.1 39.8 reduce-scatter.3
  283.0 30.9 all-gather.3
  486.3 116.0 all-gather.5
where the time goes:
time: 782 us; the launch traced here: 779 us
  blocking collectives  499 us (64%)
  local copies, waits for them, and re-layouts  117 us (15%)
  waiting for transfers between devices  109 us (14%)
  matrix products  30 us (4%)
  between operations  13.9 us (2%)
  other arithmetic  9.6 us (1%)
    all_to_all x1, blocking collectives, local(): lax.all_to_all(outgoing, 'expert', split_axis=0, concat_axis=0, tiled=True)  93.8 us
    all_to_all x1, blocking collectives, local(): lax.all_to_all(lax.all_to_all(returning, 'dp', split_axis=0, concat_axis=...  90.6 us
    unnamed x1, blocking collectives  77.6 us
    pmax x1, blocking collectives, local(): row_top = lax.pmax(row_top, ('expert', 'dp'))  75.3 us
    psum x1, blocking collectives, local(): row_total, picked = lax.psum((row_total, picked), ('expert', 'dp'))  72.7 us
    unnamed x25, local copies, waits for them, and re-layouts  53 us
    all_to_all x1, blocking collectives, local(): lax.all_to_all(returning, 'dp', split_axis=0, concat_axis=2, tiled=True)  47.4 us
    all_to_all x1, blocking collectives, local(): lax.all_to_all(lax.all_to_all(outgoing, 'expert', split_axis=0, concat_ax...  41.8 us
  transfers between devices with their start and end apart: 3, of which 3 were waited for; matrix products, arithmetic and copies ran while one was open for 0% of the time, Pallas kernels for 0%

commit v1 on v0

v1 whole, which is shorter than its diff:
```python
import functools

import jax
import jax.numpy as jnp
from jax import lax
from jax.experimental import pallas as pl
from jax.experimental.pallas import tpu as pltpu
from jax.sharding import PartitionSpec as P

MESH = pl.DeviceIdType.MESH
NY, NZ, NX = 4, 8, 4
EPSILON = 1e-06
CHUNKS = 3
SLOTS = 2
VMEM_LIMIT = 62 * 2**20

X, Z, CP, XP, HX, HC, R, T = (3 * i for i in range(8))
TS, IN, FZ, SQ, IZ, IY, FX, FYA, FYB, FC1, FC2, STZ, STY, STD = range(24, 38)
SEMS = 38

F32, BF16 = jnp.float32, jnp.bfloat16


def iota(shape, dim):
    return lax.broadcasted_iota(jnp.int32, shape, dim)


def dot(a, b):
    return jnp.dot(a, b, preferred_element_type=F32)


def kernel(
    tok_h, gain_ref, rc_ref, rr_ref, rg_ref, tg_ref, wg_h, wu_h, wd_h, fg_ref, un_h,
    out_h, lp_ref,
    tok, nb, w, wd, un, pm, um, q, qt, xs, xr, zs, za, part, crecv, xrecv, hid, rb, g,
    ts, tr, t16, ins, inr, info, sq, fs, acc, st, stz, sty, std, ssem, rsem, lsem, osem,
):
    dp = 2 * NX
    experts = NY * NZ
    e, d = lax.axis_index("expert"), lax.axis_index("dp")
    y, z = lax.div(e, NZ), lax.rem(e, NZ)
    x, c = lax.div(d, 2), lax.rem(d, 2)
    sib = d + 1 - 2 * c
    rows_tok, width = tok.shape
    blk = width // dp
    lanes = xs.shape[2]
    msg = dp * SLOTS
    rows = experts * msg
    he = experts // 2
    own = rows // dp
    units = wd.shape[0]

    def send(src, dst, idx, to):
        pltpu.make_async_remote_copy(
            src_ref=src, dst_ref=dst, send_sem=ssem.at[idx], recv_sem=rsem.at[idx],
            device_id=to, device_id_type=MESH,
        ).start()

    def landed(ref, idx):
        pltpu.make_async_copy(ref, ref, rsem.at[idx]).wait()

    def sent(ref, idx):
        pltpu.make_async_copy(ref, ref, ssem.at[idx]).wait()

    def loop(lo, hi, body):
        def step(i, carry):
            body(i)
            return carry
        lax.fori_loop(lo, hi, step, 0)

    def expert_at(i):
        dz, dy = lax.div(i, NY), lax.rem(i, NY)
        return lax.rem(y + dy, NY) * NZ + lax.rem(z + dz, NZ)

    def dp_at(i):
        return lax.rem(d + i, dp)

    def columns(k):
        return pl.ds(pl.multiple_of(k * blk, 128), blk)

    loads = [
        pltpu.make_async_copy(src, dst, lsem.at[i])
        for i, (src, dst) in enumerate([
            (tok_h, tok), (wg_h.at[0], w.at[:, pl.ds(0, units)]),
            (wu_h.at[0], w.at[:, pl.ds(units, units)]), (wd_h.at[0], wd), (un_h, un),
        ])
    ]
    for load in loads:
        load.start()
    barrier = pltpu.get_barrier_semaphore()

    def greet_dp(i):
        pl.semaphore_signal(barrier, inc=1, device_id=(e, dp_at(i)), device_id_type=MESH)

    def greet_expert(i):
        pl.semaphore_signal(barrier, inc=1, device_id=(expert_at(i), d), device_id_type=MESH)

    loop(1, experts, greet_expert)
    loop(1, dp, greet_dp)

    ec, er = rc_ref[...].astype(F32), rr_ref[...].astype(F32)
    same = ec == er
    before, after = iota(same.shape, 0), iota(same.shape, 1)
    rank_row = jnp.sum(jnp.where(same & (before < after), 1.0, 0.0), axis=0, keepdims=True)
    rank_col = jnp.sum(jnp.where(same & (after < before), 1.0, 0.0), axis=1, keepdims=True)

    def slot_of(rank, expert):
        chunk = jnp.floor(rank * (1.0 / SLOTS))
        return chunk * lanes + expert * SLOTS + (rank - chunk * SLOTS)

    pm[...] = jnp.where(iota(pm.shape, 0).astype(F32) == slot_of(rank_row, er), 1.0, 0.0).astype(BF16)
    um[...] = jnp.where(iota(um.shape, 1).astype(F32) == slot_of(rank_col, ec), 1.0, 0.0).astype(BF16)

    lane = iota((msg, 128), 1)
    row = iota((msg, 128), 0)
    base = jnp.where(
        lane == 1, ec[:msg] * msg + (d * SLOTS).astype(F32) + rank_col[:msg],
        jnp.where(lane == 2, rg_ref[0:msg, :], 0.0),
    )
    first = jnp.where(lane == 0, tg_ref[0].astype(F32), base[0:1])
    second = jnp.where(lane == 0, tg_ref[1].astype(F32), base[1:2])
    ins[...] = jnp.where(row == 2 * d, first, jnp.where(row == 2 * d + 1, second, 0.0))
    inr[d] = ins[...]

    loads[0].wait()
    tile = min(16, rows_tok)

    def norm(i):
        at = pl.ds(pl.multiple_of(i * tile, tile), tile)
        wide = tok[at, :].astype(F32)
        mean_sq = jnp.mean(wide * wide, axis=-1, keepdims=True)
        nb[at, :] = (wide * lax.rsqrt(mean_sq + EPSILON) * gain_ref[...]).astype(BF16)

    loop(0, rows_tok // tile, norm)

    def place(ch):
        def body(k):
            xs[ch, k] = dot(pm[ch * lanes:(ch + 1) * lanes, :], nb[:, columns(k)]).astype(BF16)
        loop(0, dp, body)
        xr[ch, d] = xs[ch, d]

    def place_send(ch):
        def body(i):
            send(xs.at[ch, dp_at(i)], xr.at[ch, d], X + ch, (e, dp_at(i)))
        loop(1, dp, body)

    place(0)
    pl.semaphore_wait(barrier, experts - 1 + dp - 1)
    place_send(0)

    def scored_tokens(k):
        r16 = iota((msg, blk), 0)
        top = tok[0:msg, columns(k)].astype(F32)
        ts[k] = jnp.where(r16 == 2 * d, top[0:1], jnp.where(r16 == 2 * d + 1, top[1:2], 0.0)).astype(BF16)

    loop(0, dp, scored_tokens)
    tr[d] = ts[d]
    loop(1, dp, lambda i: send(ins, inr.at[d], IN, (e, dp_at(i))))
    loop(1, dp, lambda i: send(ts.at[dp_at(i)], tr.at[d], TS, (e, dp_at(i))))
    for ch in range(1, CHUNKS):
        place(ch)
        place_send(ch)

    part_rows = rows // 8

    def permutations(i):
        at = pl.ds(pl.multiple_of(i * part_rows, part_rows), part_rows)
        a = iota((part_rows, rows), 0) + i * part_rows
        b = iota((part_rows, rows), 1)
        ex, dev, slot = lax.div(a, msg), lax.rem(lax.div(a, SLOTS), dp), lax.rem(a, SLOTS)
        q[at, :] = jnp.where(b == dev * lanes + ex * SLOTS + slot, 1.0, 0.0).astype(BF16)
        ex, dev = lax.rem(lax.div(a, SLOTS), experts), lax.div(a, lanes)
        qt[at, :] = jnp.where(b == ex * msg + dev * SLOTS + slot, 1.0, 0.0).astype(BF16)

    loop(0, 8, permutations)

    def dispatch(ch):
        landed(xr.at[ch, pl.ds(0, dp - 1)], X + ch)

        def body(i):
            at = pl.ds(pl.multiple_of(i * (rows // 2), rows // 2), rows // 2)
            moved = dot(q[at, :], xr[ch].reshape(rows, blk)).astype(BF16)
            zs[ch, pl.ds(i * he, he)] = moved.reshape(he, msg, blk)
        loop(0, 2, body)
        za[ch, e] = zs[ch, e]
        loop(1, experts, lambda i: send(zs.at[ch, expert_at(i)], za.at[ch, e], Z + ch, (expert_at(i), d)))

    dispatch(0)
    for load in loads[1:]:
        load.wait()
    landed(inr.at[pl.ds(0, dp - 1)], IN)
    landed(tr.at[pl.ds(0, dp - 1)], TS)
    total = inr[0]
    tokens16 = tr[0].astype(F32)
    for k in range(1, dp):
        total = total + inr[k]
        tokens16 = tokens16 + tr[k].astype(F32)
    ins_total = total
    t16[...] = tokens16
    dispatch(1)
    dispatch(2)

    def gate_up(ch):
        landed(za.at[ch, pl.ds(0, experts - 1)], Z + ch)
        step = min(256, units)

        def half(p):
            def body(n):
                at = pl.ds(pl.multiple_of(n * step, step), step)
                values = za[ch, pl.ds(p * he, he)].reshape(he * msg, blk)
                part[ch, p, :, at] = dot(values, w[:, at]).astype(BF16)
            loop(0, 2 * units // step, body)

        half(1 - c)
        send(part.at[ch, 1 - c], crecv.at[ch], CP + ch, (e, sib))
        half(c)
        landed(crecv.at[ch], CP + ch)

        def add(i):
            to = lax.rem(x + i, NX)
            at = pl.ds(pl.multiple_of(to * own, own), own)
            part[ch, c, at, :] = (part[ch, c, at, :].astype(F32) + crecv[ch, at, :].astype(F32)).astype(BF16)
            return to, at

        def body(i):
            to, at = add(i)
            send(part.at[ch, c, at, :], xrecv.at[ch, i - 1], XP + ch, (e, 2 * to + c))
        loop(1, NX, body)
        add(0)

    def activate(ch):
        landed(xrecv.at[ch], XP + ch)
        at = pl.ds(pl.multiple_of(x * own, own), own)
        summed = part[ch, c, at, :].astype(F32)
        for i in range(NX - 1):
            summed = summed + xrecv[ch, i].astype(F32)
        gate, up = summed[:, :units], summed[:, units:]
        hid[ch, c, x] = (gate / (1.0 + jnp.exp(-gate)) * up).astype(BF16)
        loop(1, NX, lambda i: send(hid.at[ch, c, x], hid.at[ch, c, x], HX + ch, (e, 2 * lax.rem(x + i, NX) + c)))

    def share(ch):
        landed(hid.at[ch, c, pl.ds(0, NX - 1)], HX + ch)
        send(hid.at[ch, c], hid.at[ch, c], HC + ch, (e, sib))

    def down(ch):
        sent(zs.at[ch, pl.ds(0, experts - 1)], Z + ch)

        def body(i):
            p = c + i - 2 * c * i

            @pl.when(i == 1)
            def _():
                landed(hid.at[ch, c], HC + ch)

            result = dot(hid[ch, p].reshape(he * msg, units), wd[...]).astype(BF16)
            zs[ch, pl.ds(p * he, he)] = result.reshape(he, msg, blk)

            def give(j):
                to = p * he + lax.rem(j + e, he)

                @pl.when(to != e)
                def _():
                    send(zs.at[ch, to], rb.at[ch, e], R + ch, (to, d))
            loop(0, he, give)
        loop(0, 2, body)
        rb[ch, e] = zs[ch, e]

    def back(ch):
        landed(rb.at[ch, pl.ds(0, experts - 1)], R + ch)

    def home(ch):
        sent(xs.at[ch, pl.ds(0, dp - 1)], X + ch)

        def body(i):
            at = pl.ds(pl.multiple_of(i * (rows // 2), rows // 2), rows // 2)
            moved = dot(qt[at, :], rb[ch].reshape(rows, blk)).astype(BF16)
            xs[ch, pl.ds(i * (dp // 2), dp // 2)] = moved.reshape(dp // 2, lanes, blk)
        loop(0, 2, body)
        g[d, ch * lanes:(ch + 1) * lanes, :] = xs[ch, d]
        loop(1, dp, lambda i: send(
            xs.at[ch, dp_at(i)], g.at[d, pl.ds(ch * lanes, lanes), :], T + ch, (e, dp_at(i))))

    def score_rows():
        slot, scale = ins_total[:, 1:2], ins_total[:, 2:3]
        pick = jnp.where(iota((msg, rows), 1).astype(F32) == slot, 1.0, 0.0).astype(BF16)
        picked = dot(pick, rb[0].reshape(rows, blk))
        layer = (t16[...] + scale * picked).astype(BF16).astype(F32)
        fs[c, y, x, z] = (layer * fg_ref[:, columns(d)]).astype(BF16)
        loop(1, NZ, lambda i: send(
            fs.at[c, y, x, z], fs.at[c, y, x, z], FZ, (y * NZ + lax.rem(z + i, NZ), d)))
        squares = jnp.sum(layer * layer, axis=-1, keepdims=True)
        sq[d] = jnp.broadcast_to(squares, (msg, 128))
        loop(1, dp, lambda i: send(sq.at[d], sq.at[d], SQ, (e, dp_at(i))))

    def score_info():
        landed(sq.at[pl.ds(0, dp - 1)], SQ)
        squares = sq[0]
        for k in range(1, dp):
            squares = squares + sq[k]
        info[y, z] = jnp.where(lane == 1, squares, ins_total)
        loop(1, NZ, lambda i: send(info.at[y, z], info.at[y, z], IZ, (y * NZ + lax.rem(z + i, NZ), d)))

    def to_y(i):
        return (lax.rem(y + i, NY) * NZ + z, d)

    def score_x():
        landed(fs.at[c, y, x, pl.ds(0, NZ - 1)], FZ)
        piece = fs.at[c, y, x]
        loop(1, NX, lambda i: send(piece, piece, FX, (e, 2 * lax.rem(x + i, NX) + c)))
        loop(1, NY, lambda i: send(piece, piece, FYA, to_y(i)))
        landed(info.at[y, pl.ds(0, NZ - 1)], IZ)
        loop(1, NY, lambda i: send(info.at[y], info.at[y], IY, to_y(i)))

    def score_y():
        landed(fs.at[c, y, pl.ds(0, NX - 1)], FX)

        def body(j):
            piece = fs.at[c, y, lax.rem(x + j, NX)]
            loop(1, NY, lambda i: send(piece, piece, FYB, to_y(i)))
        loop(1, NX, body)
        send(fs.at[c, y], fs.at[c, y], FC1, (e, sib))

    def score_core():
        landed(fs.at[c, pl.ds(0, NY - 1), 0], FYA)
        landed(fs.at[c, pl.ds(0, NY - 1), pl.ds(0, NX - 1)], FYB)

        def body(i):
            piece = fs.at[c, lax.rem(y + i, NY)]
            send(piece, piece, FC2, (e, sib))
        loop(1, NY, body)

    def logits_half(p, start):
        def body(i):
            values = fs[p, :, i].reshape(rows, blk)
            product = lax.dot_general(
                un[:, columns(2 * i + p)], values, (((1,), (1,)), ((), ())), preferred_element_type=F32)
            acc[...] += product
        if start:
            acc[...] = jnp.zeros_like(acc)
        loop(0, NX, body)

    def combine(ref, n):
        top = ref[0, 0:1]
        for k in range(1, n):
            top = jnp.maximum(top, ref[k, 0:1])
        total = jnp.zeros_like(top)
        picked = jnp.zeros_like(top)
        for k in range(n):
            total = total + ref[k, 1:2] * jnp.exp(ref[k, 0:1] - top)
            picked = picked + ref[k, 2:3]
        return top, total, picked

    def put(ref, at, stats):
        r8 = iota(ref.shape[1:], 0)
        ref[at] = jnp.where(r8 == 0, stats[0], jnp.where(r8 == 1, stats[1], jnp.where(r8 == 2, stats[2], 0.0)))

    def score_logits():
        logits_half(c, True)
        landed(fs.at[c, 0], FC1)
        landed(fs.at[c, pl.ds(0, NY - 1)], FC2)
        logits_half(1 - c, False)
        landed(info.at[pl.ds(0, NY - 1)], IY)
        known = info[...].reshape(rows, 128).T
        target, squares = known[0:1], known[1:2]
        logits = acc[...] * lax.rsqrt(squares * (1.0 / width) + EPSILON)
        top = jnp.max(logits, axis=0, keepdims=True)
        total = jnp.sum(jnp.exp(logits - top), axis=0, keepdims=True)
        entry = iota(logits.shape, 0) + (e * dp + d) * logits.shape[0]
        picked = jnp.sum(jnp.where(entry.astype(F32) == target, logits, 0.0), axis=0, keepdims=True)
        put(stz, z, (top, total, picked))
        loop(1, NZ, lambda i: send(stz.at[z], stz.at[z], STZ, (y * NZ + lax.rem(z + i, NZ), d)))

    def score_stats_y():
        landed(stz.at[pl.ds(0, NZ - 1)], STZ)
        put(sty, y, combine(stz, NZ))
        loop(1, NY, lambda i: send(sty.at[y], sty.at[y], STY, to_y(i)))

    def score_stats_dp():
        landed(sty.at[pl.ds(0, NY - 1)], STY)
        put(std, d, combine(sty, NY))
        loop(1, dp, lambda i: send(std.at[d], std.at[d], STD, (e, dp_at(i))))

    def score_end():
        landed(std.at[pl.ds(0, dp - 1)], STD)
        top, total, picked = combine(std, dp)
        lp_ref[...] = picked - (top + jnp.log(total))

    def finish():
        for ch in range(CHUNKS):
            landed(g.at[pl.ds(0, dp - 1), pl.ds(0, lanes), :], T + ch)

        def body(k):
            at = columns(k)
            picked = dot(um[...], g[k])
            tok[:, at] = (tok[:, at].astype(F32) + rg_ref[...] * picked).astype(BF16)
            pltpu.make_async_copy(tok.at[:, at], out_h.at[:, at], osem).start()
        loop(0, dp, body)

    gate_up(0)
    activate(0)
    gate_up(1)
    share(0)
    down(0)
    activate(1)
    share(1)
    down(1)
    gate_up(2)
    back(0)
    score_rows()
    home(0)
    score_info()
    score_x()
    activate(2)
    share(2)
    score_y()
    down(2)
    back(1)
    home(1)
    back(2)
    home(2)
    score_core()
    score_logits()
    score_stats_y()
    finish()
    score_stats_dp()
    score_end()

    pltpu.make_async_copy(tok, out_h, osem).wait()
    for ch in range(CHUNKS):
        sent(part.at[ch, 0], CP + ch)
        sent(xrecv.at[ch], XP + ch)
        sent(hid.at[ch, 0, pl.ds(0, NX - 1)], HX + ch)
        sent(hid.at[ch, 0], HC + ch)
        sent(zs.at[ch, pl.ds(0, experts - 1)], R + ch)
        sent(xs.at[ch, pl.ds(0, dp - 1)], T + ch)
    sent(inr.at[pl.ds(0, dp - 1)], IN)
    sent(tr.at[pl.ds(0, dp - 1)], TS)
    sent(fs.at[0, 0, 0, pl.ds(0, NZ - 1)], FZ)
    sent(sq.at[pl.ds(0, dp - 1)], SQ)
    sent(info.at[0, pl.ds(0, NZ - 1)], IZ)
    sent(info.at[pl.ds(0, NY - 1)], IY)
    sent(fs.at[0, 0, pl.ds(0, NX - 1)], FX)
    sent(fs.at[0, pl.ds(0, NY - 1), 0], FYA)
    sent(fs.at[0, pl.ds(0, NY - 1), pl.ds(0, NX - 1)], FYB)
    sent(fs.at[0, 0], FC1)
    sent(fs.at[0, pl.ds(0, NY - 1)], FC2)
    sent(stz.at[pl.ds(0, NZ - 1)], STZ)
    sent(sty.at[pl.ds(0, NY - 1)], STY)
    sent(std.at[pl.ds(0, dp - 1)], STD)


def local(
    tokens, norm_gain, routing, route_gate, gate_weight, up_weight, down_weight,
    final_gain, unembed, targets,
):
    rows_tok, width = tokens.shape
    dp, experts = 2 * NX, NY * NZ
    blk, units, vocab = width // dp, up_weight.shape[2], unembed.shape[0]
    lanes, msg = experts * SLOTS, dp * SLOTS
    rows = experts * msg
    own = rows // dp
    vmem = pl.BlockSpec(memory_space=pltpu.VMEM)
    hbm = pl.BlockSpec(memory_space=pl.ANY)
    smem = pl.BlockSpec(memory_space=pltpu.SMEM)
    layer_out, log_probs = pl.pallas_call(
        kernel,
        out_shape=(
            jax.ShapeDtypeStruct((rows_tok, width), BF16),
            jax.ShapeDtypeStruct((1, rows), F32),
        ),
        in_specs=[hbm, vmem, vmem, vmem, vmem, smem, hbm, hbm, hbm, vmem, hbm],
        out_specs=(hbm, vmem),
        scratch_shapes=[
            pltpu.VMEM((rows_tok, width), BF16),
            pltpu.VMEM((rows_tok, width), BF16),
            pltpu.VMEM((blk, 2 * units), BF16),
            pltpu.VMEM((units, blk), BF16),
            pltpu.VMEM((vocab, width), BF16),
            pltpu.VMEM((CHUNKS * lanes, rows_tok), BF16),
            pltpu.VMEM((rows_tok, CHUNKS * lanes), BF16),
            pltpu.VMEM((rows, rows), BF16),
            pltpu.VMEM((rows, rows), BF16),
            pltpu.VMEM((CHUNKS, dp, lanes, blk), BF16),
            pltpu.VMEM((CHUNKS, dp, lanes, blk), BF16),
            pltpu.VMEM((CHUNKS, experts, msg, blk), BF16),
            pltpu.VMEM((CHUNKS, experts, msg, blk), BF16),
            pltpu.VMEM((CHUNKS, 2, rows // 2, 2 * units), BF16),
            pltpu.VMEM((CHUNKS, rows // 2, 2 * units), BF16),
            pltpu.VMEM((CHUNKS, NX - 1, own, 2 * units), BF16),
            pltpu.VMEM((CHUNKS, 2, NX, own, units), BF16),
            pltpu.VMEM((CHUNKS, experts, msg, blk), BF16),
            pltpu.VMEM((dp, CHUNKS * lanes, blk), BF16),
            pltpu.VMEM((dp, msg, blk), BF16),
            pltpu.VMEM((dp, msg, blk), BF16),
            pltpu.VMEM((msg, blk), F32),
            pltpu.VMEM((msg, 128), F32),
            pltpu.VMEM((dp, msg, 128), F32),
            pltpu.VMEM((NY, NZ, msg, 128), F32),
            pltpu.VMEM((dp, msg, 128), F32),
            pltpu.VMEM((2, NY, NX, NZ, msg, blk), BF16),
            pltpu.VMEM((vocab, rows), F32),
            pltpu.VMEM((8, rows), F32),
            pltpu.VMEM((NZ, 8, rows), F32),
            pltpu.VMEM((NY, 8, rows), F32),
            pltpu.VMEM((dp, 8, rows), F32),
            pltpu.SemaphoreType.DMA((SEMS,)),
            pltpu.SemaphoreType.DMA((SEMS,)),
            pltpu.SemaphoreType.DMA((5,)),
            pltpu.SemaphoreType.DMA,
        ],
        compiler_params=pltpu.CompilerParams(
            collective_id=0, has_side_effects=True, vmem_limit_bytes=VMEM_LIMIT
        ),
        name="routed_layer",
    )(
        tokens, norm_gain.reshape(1, width), routing, routing.reshape(1, rows_tok),
        route_gate.reshape(rows_tok, 1), targets, gate_weight, up_weight, down_weight,
        final_gain.reshape(1, width), unembed,
    )
    return layer_out, log_probs.reshape(rows)


def solution(mesh):
    placed = (
        P(("expert", "dp"), None),
        P(),
        P(("expert", "dp"), None),
        P(("expert", "dp")),
        P("expert", "dp", None),
        P("expert", "dp", None),
        P("expert", None, "dp"),
        P(),
        P(("expert", "dp"), None),
        P(("expert", "dp")),
    )
    return jax.shard_map(
        local,
        mesh=mesh,
        in_specs=placed,
        out_specs=(P(("expert", "dp"), None), P()),
        check_vma=False,
    )
```

time: 782 us -> 222 us (0.28)
  blocking collectives: 499 us -> 0 us
  Pallas kernels: 0 us -> 215 us
  local copies, waits for them, and re-layouts: 117 us -> 6.19 us
  waiting for transfers between devices: 109 us -> 0 us
  matrix products: 30 us -> 0 us
  between operations: 13.9 us -> 0.65 us
  other arithmetic: 9.6 us -> 0 us
    all_to_all x4 -> x0, blocking collectives: 274 us -> none  [the longest x1 93.8 us: local(): lax.all_to_all(outgoing, 'expert', split_axis=0, concat_axis=0, tiled=True)]
    pallas_call x0 -> x1, Pallas kernels: none -> 215 us  [local(): pl.pallas_call(kernel, out_shape=(jax.ShapeDtypeStruct((rows_tok, width),...]
    unnamed x1 -> x0, blocking collectives: 77.6 us -> none
    pmax x1 -> x0, blocking collectives: 75.3 us -> none  [local(): row_top = lax.pmax(row_top, ('expert', 'dp'))]
    psum x1 -> x0, blocking collectives: 72.7 us -> none  [local(): row_total, picked = lax.psum((row_total, picked), ('expert', 'dp'))]
    all_gather x2 -> x0, waiting for transfers between devices: 69.4 us -> none  [the longest x1 38.3 us: local(): lax.all_gather(final_local, ('expert', 'dp'), axis=0, tiled=True)]
    unnamed x25 -> x5, local copies, waits for them, and re-layouts: 53 us -> 4.82 us
    all_to_all x5 -> x0, local copies, waits for them, and re-layouts: 42.8 us -> none  [the longest x1 15.6 us: local(): lax.all_to_all(outgoing, 'expert', split_axis=0, concat_axis=0, tiled=True)]
  transfers between devices with their start and end apart: 3 -> 0, of which waited for: 3 -> 0; matrix products, arithmetic and copies ran while one was open for 0% -> 0% of each run, Pallas kernels for 0% -> 0%
where the time goes in v1:
time: 222 us
  Pallas kernels  215 us (97%)
  local copies, waits for them, and re-layouts  6.19 us (3%)
    pallas_call x1, Pallas kernels, local(): pl.pallas_call(kernel, out_shape=(jax.ShapeDtypeStruct((rows_tok, width),...  215 us
    unnamed x5, local copies, waits for them, and re-layouts  4.82 us

profile of v1, /device:TPU:1, one launch (start us, length us, event | category | flops | bytes accessed | tf_op | source)
XLA Modules:
  0.0 222.0 jit_solution(13736384579113769057)
XLA Ops:
  0.6 1.4 copy.13.rg_ref
  2.0 1.4 copy.12.rc_ref
  3.4 215.2 %routed_layer.1 = (bf16[128,7168]{1,0:T(8,128)(2,1)}, f32[1,512]{1,0:T(1,128)}) custom-call(bf16[128,7168]{1,0:T(8,128)(2,1)} %tok_h.1, f32[1,7168]{1,0:T(1,128)} %bitcast.5, s32[128,1]{1,0:T(8,128)} %copy.12.rc_ref, s32[1,128]{1,0:T(1,128)} %bitcast.7, f32[128,1]{1,0:T(8,128)} %copy.13.rg_ref, s32[2]{0:T(128)} %tg_ref.1, bf16[1,896,1024]{2,1,0:T(8,128)(2,1)} %wg_h.1, ...), custom_call_target="tpu_custom_call" | custom-call | tf_op jit(solution)/shard_map/routed_layer/pallas_call | solution.py:465
  218.6 0.0 copy-start
  218.6 2.8 %copy.16 = bf16[128,7168]{1,0:T(8,128)(2,1)} copy(bf16[128,7168]{1,0:T(8,128)(2,1)} %get-tuple-element.8) | data formatting | bytes 3670016
  221.5 0.0 copy-done
  221.5 0.6 copy.17
Async XLA Ops:
  218.6 2.9 %copy-start = (f32[1,512]{1,0:T(1,128)S(1)}, f32[1,512]{1,0:T(1,128)}, u32[]{:S(2)}) copy-start(f32[1,512]{1,0:T(1,128)} %get-tuple-element.5) | copy-start | bytes 6148

commit v2 on v1

v2 whole, which is shorter than its diff:
```python
import functools

import jax
import jax.numpy as jnp
from jax import lax
from jax.experimental import pallas as pl
from jax.experimental.pallas import tpu as pltpu
from jax.sharding import PartitionSpec as P

MESH = pl.DeviceIdType.MESH
NY, NZ, NX = 4, 8, 4
EPSILON = 1e-06
CHUNKS = 3
SLOTS = 2
VMEM_LIMIT = 62 * 2**20

X, CP, XP, HX, HC = (6 * i for i in range(5))
Z, R, T = 30, 33, 36
TS, IN, FZ, SQ, IZ, IY, FX, FYA, FYB, FC1, FC2, STZ, STY, STD = range(39, 53)
SEMS = 53

F32, BF16 = jnp.float32, jnp.bfloat16


def iota(shape, dim):
    return lax.broadcasted_iota(jnp.int32, shape, dim)


def dot(a, b):
    return jnp.dot(a, b, preferred_element_type=F32)


def kernel(
    tok_h, gain_ref, rr_ref, rgr_ref, tg_ref, wg_h, wu_h, wd_h, fg_ref, un_h,
    out_h, lp_ref,
    rg_ref, tok, nb, w, wd, un, pm, um, q, qt, xs, xr, zs, za, part, crecv, xrecv, hid, rb, g,
    ts, tr, t16, it16, ins, inr, info, sq, fs, acc, st, stz, sty, std, ssem, rsem, lsem, osem,
):
    dp = 2 * NX
    experts = NY * NZ
    e, d = lax.axis_index("expert"), lax.axis_index("dp")
    y, z = lax.div(e, NZ), lax.rem(e, NZ)
    x, c = lax.div(d, 2), lax.rem(d, 2)
    sib = d + 1 - 2 * c
    rows_tok, width = tok.shape
    blk = width // dp
    half_lanes = xs.shape[3]
    lanes = 2 * half_lanes
    msg = dp * SLOTS
    rows = experts * msg
    he = experts // 2
    own = rows // dp
    units = wd.shape[0]
    hu = units // 2
    zh = NZ // 2
    place_me = lax.rem(z, 2) * he + y * zh + lax.div(z, 2)
    f_me, s_me = x * (1 - c) + y * c, y * (1 - c) + x * c

    def send(src, dst, idx, to):
        pltpu.make_async_remote_copy(
            src_ref=src, dst_ref=dst, send_sem=ssem.at[idx], recv_sem=rsem.at[idx],
            device_id=to, device_id_type=MESH,
        ).start()

    def landed(ref, idx):
        pltpu.make_async_copy(ref, ref, rsem.at[idx]).wait()

    pending = {}

    def later(ref, idx):
        pending[idx] = ref

    def sent(idx):
        ref = pending.pop(idx)
        pltpu.make_async_copy(ref, ref, ssem.at[idx]).wait()

    def loop(lo, hi, body):
        def step(i, carry):
            body(i)
            return carry
        lax.fori_loop(lo, hi, step, 0)

    def expert_at(i):
        dz, dy = lax.div(i, NY), lax.rem(i, NY)
        return lax.rem(y + dy, NY) * NZ + lax.rem(z + dz, NZ)

    def dp_at(i):
        return lax.rem(d + i, dp)

    def columns(k):
        return pl.ds(pl.multiple_of(k * blk, 128), blk)

    loads = [
        pltpu.make_async_copy(src, dst, lsem.at[i])
        for i, (src, dst) in enumerate([
            (tok_h, tok),
            (wg_h.at[0, :, pl.ds(0, hu)], w.at[0, :, pl.ds(0, hu)]),
            (wu_h.at[0, :, pl.ds(0, hu)], w.at[0, :, pl.ds(hu, hu)]),
            (wg_h.at[0, :, pl.ds(hu, hu)], w.at[1, :, pl.ds(0, hu)]),
            (wu_h.at[0, :, pl.ds(hu, hu)], w.at[1, :, pl.ds(hu, hu)]),
            (wd_h.at[0], wd), (un_h, un),
        ])
    ]
    for load in loads:
        load.start()
    barrier = pltpu.get_barrier_semaphore()

    def greet_dp(i):
        pl.semaphore_signal(barrier, inc=1, device_id=(e, dp_at(i)), device_id_type=MESH)

    def greet_expert(i):
        pl.semaphore_signal(barrier, inc=1, device_id=(expert_at(i), d), device_id_type=MESH)

    loop(1, experts, greet_expert)
    loop(1, dp, greet_dp)

    def column(values):
        n = values.shape[1]
        return jnp.sum(jnp.where(iota((n, n), 0) == iota((n, n), 1), values, 0.0), axis=1, keepdims=True)

    er = rr_ref[...].astype(F32)
    ec = column(er)
    rg_ref[...] = column(rgr_ref[...])
    same = ec == er
    before, after = iota(same.shape, 0), iota(same.shape, 1)
    rank_row = jnp.sum(jnp.where(same & (before < after), 1.0, 0.0), axis=0, keepdims=True)
    rank_col = jnp.sum(jnp.where(same & (after < before), 1.0, 0.0), axis=1, keepdims=True)

    def place_of(expert):
        at_y = jnp.floor(expert * (1.0 / NZ))
        at_z = expert - at_y * NZ
        half_z = jnp.floor(at_z * 0.5)
        return (at_z - 2.0 * half_z) * he + at_y * zh + half_z

    def slot_of(rank, expert):
        chunk = jnp.floor(rank * (1.0 / SLOTS))
        return chunk * lanes + place_of(expert) * SLOTS + (rank - chunk * SLOTS)

    pm[...] = jnp.where(iota(pm.shape, 0).astype(F32) == slot_of(rank_row, er), 1.0, 0.0).astype(BF16)
    um[...] = jnp.where(iota(um.shape, 1).astype(F32) == slot_of(rank_col, ec), 1.0, 0.0).astype(BF16)

    lane = iota((msg, 128), 1)
    row = iota((msg, 128), 0)
    base = jnp.where(
        lane == 1, place_of(ec[:msg]) * msg + (d * SLOTS).astype(F32) + rank_col[:msg],
        jnp.where(lane == 2, rg_ref[0:msg, :], 0.0),
    )
    first = jnp.where(lane == 0, tg_ref[0].astype(F32), base[0:1])
    second = jnp.where(lane == 0, tg_ref[1].astype(F32), base[1:2])
    ins[...] = jnp.where(row == 2 * d, first, jnp.where(row == 2 * d + 1, second, 0.0))
    inr[d] = ins[...]

    loads[0].wait()
    tile = min(16, rows_tok)

    def norm(i):
        at = pl.ds(pl.multiple_of(i * tile, tile), tile)
        wide = tok[at, :].astype(F32)
        mean_sq = jnp.mean(wide * wide, axis=-1, keepdims=True)
        nb[at, :] = (wide * lax.rsqrt(mean_sq + EPSILON) * gain_ref[...]).astype(BF16)

    loop(0, rows_tok // tile, norm)

    def place(ch):
        def body(k):
            values = dot(pm[ch * lanes:(ch + 1) * lanes, :], nb[:, columns(k)]).astype(BF16)
            xs[ch, 0, k] = values[:half_lanes]
            xs[ch, 1, k] = values[half_lanes:]
        loop(0, dp, body)

    def place_send(ch):
        for h in range(2):
            def body(i):
                send(xs.at[ch, h, dp_at(i)], xr.at[ch, h, d], X + 2 * ch + h, (e, dp_at(i)))
            loop(1, dp, body)
            later(xr.at[ch, h, pl.ds(0, dp - 1)], X + 2 * ch + h)
            xr[ch, h, d] = xs[ch, h, d]

    half_rows = rows // 2

    def permutations():
        a, b = iota((half_rows, half_rows), 0), iota((half_rows, half_rows), 1)
        ex, dev, slot = lax.div(a, msg), lax.rem(lax.div(a, SLOTS), dp), lax.rem(a, SLOTS)
        q[...] = jnp.where(b == dev * half_lanes + ex * SLOTS + slot, 1.0, 0.0).astype(BF16)
        ex, dev = lax.rem(lax.div(a, SLOTS), he), lax.div(a, half_lanes)
        qt[...] = jnp.where(b == ex * msg + dev * SLOTS + slot, 1.0, 0.0).astype(BF16)

    def scored_tokens(k):
        r16 = iota((msg, blk), 0)
        top = tok[0:msg, columns(k)].astype(F32)
        ts[k] = jnp.where(r16 == 2 * d, top[0:1], jnp.where(r16 == 2 * d + 1, top[1:2], 0.0)).astype(BF16)

    def dispatch(ch):
        for h in range(2):
            landed(xr.at[ch, h, pl.ds(0, dp - 1)], X + 2 * ch + h)
            moved = dot(q[...], xr[ch, h].reshape(half_rows, blk)).astype(BF16)
            zs[ch, h * he:(h + 1) * he] = moved.reshape(he, msg, blk)
            shift = lax.rem(z + h, 2)

            def body(i):
                to_y, to_z = lax.rem(y + lax.rem(i, NY), NY), lax.rem(z + 2 * lax.div(i, NY) + shift, NZ)
                at = h * he + to_y * zh + lax.div(to_z, 2)
                send(zs.at[ch, at], za.at[ch, e], Z + ch, (to_y * NZ + to_z, d))
            loop(1 - shift, he, body)
        later(za.at[ch, pl.ds(0, experts - 1)], Z + ch)
        za[ch, e] = zs[ch, place_me]

    place(0)
    permutations()
    pl.semaphore_wait(barrier, experts - 1 + dp - 1)
    place_send(0)
    place(1)
    place_send(1)
    loop(0, dp, scored_tokens)
    tr[d] = ts[d]
    dispatch(0)
    place(2)
    place_send(2)
    loop(1, dp, lambda i: send(ins, inr.at[d], IN, (e, dp_at(i))))
    loop(1, dp, lambda i: send(ts.at[dp_at(i)], tr.at[d], TS, (e, dp_at(i))))
    later(inr.at[pl.ds(0, dp - 1)], IN)
    later(tr.at[pl.ds(0, dp - 1)], TS)
    for load in loads[1:]:
        load.wait()
    dispatch(1)
    landed(inr.at[pl.ds(0, dp - 1)], IN)
    landed(tr.at[pl.ds(0, dp - 1)], TS)
    ins_total = inr[0]
    tokens16 = tr[0].astype(F32)
    for k in range(1, dp):
        ins_total = ins_total + inr[k]
        tokens16 = tokens16 + tr[k].astype(F32)
    t16[...] = tokens16
    it16[...] = ins_total
    dispatch(2)

    def gate_up(ch):
        landed(za.at[ch, pl.ds(0, experts - 1)], Z + ch)
        step = min(256, hu)

        def half(p, u):
            def body(n):
                at = pl.ds(pl.multiple_of(n * step, step), step)
                values = za[ch, pl.ds(p * he, he)].reshape(he * msg, blk)
                part[ch, u, p, :, at] = dot(values, w[u, :, at]).astype(BF16)
            loop(0, 2 * hu // step, body)

        for u in range(2):
            half(1 - c, u)
            send(part.at[ch, u, 1 - c], crecv.at[ch, u], CP + 2 * ch + u, (e, sib))
            later(crecv.at[ch, u], CP + 2 * ch + u)
        for u in range(2):
            half(c, u)
            landed(crecv.at[ch, u], CP + 2 * ch + u)

            def add(i):
                to = lax.rem(x + i, NX)
                at = pl.ds(pl.multiple_of(to * own, own), own)
                part[ch, u, c, at, :] = (
                    part[ch, u, c, at, :].astype(F32) + crecv[ch, u, at, :].astype(F32)).astype(BF16)
                return to, at

            def body(i):
                to, at = add(i)
                send(part.at[ch, u, c, at, :], xrecv.at[ch, u, i - 1], XP + 2 * ch + u, (e, 2 * to + c))
            loop(1, NX, body)
            add(0)
            later(xrecv.at[ch, u], XP + 2 * ch + u)

    def activate(ch, u):
        landed(xrecv.at[ch, u], XP + 2 * ch + u)
        at = pl.ds(pl.multiple_of(x * own, own), own)
        summed = part[ch, u, c, at, :].astype(F32)
        for i in range(NX - 1):
            summed = summed + xrecv[ch, u, i].astype(F32)
        gate, up = summed[:, :hu], summed[:, hu:]
        hid[ch, u, c, x] = (gate / (1.0 + jnp.exp(-gate)) * up).astype(BF16)
        mine = hid.at[ch, u, c, x]
        loop(1, NX, lambda i: send(mine, mine, HX + 2 * ch + u, (e, 2 * lax.rem(x + i, NX) + c)))
        later(hid.at[ch, u, 0, pl.ds(0, NX - 1)], HX + 2 * ch + u)

    def share(ch, u):
        landed(hid.at[ch, u, c, pl.ds(0, NX - 1)], HX + 2 * ch + u)
        send(hid.at[ch, u, c], hid.at[ch, u, c], HC + 2 * ch + u, (e, sib))
        later(hid.at[ch, u, 0], HC + 2 * ch + u)

    def down(ch):
        sent(Z + ch)

        def body(i):
            p = c + i - 2 * c * i

            @pl.when(i == 1)
            def _():
                for u in range(2):
                    landed(hid.at[ch, u, c], HC + 2 * ch + u)

            result = dot(hid[ch, 0, p].reshape(he * msg, hu), wd[:hu, :])
            result += dot(hid[ch, 1, p].reshape(he * msg, hu), wd[hu:, :])
            zs[ch, pl.ds(p * he, he)] = result.astype(BF16).reshape(he, msg, blk)

            def give(j):
                to = p * he + lax.rem(j + e, he)

                @pl.when(to != e)
                def _():
                    send(zs.at[ch, to], rb.at[ch, place_me], R + ch, (to, d))
            loop(0, he, give)
        loop(0, 2, body)
        rb[ch, place_me] = zs[ch, e]
        later(rb.at[ch, pl.ds(0, experts - 1)], R + ch)

    def back(ch):
        landed(rb.at[ch, pl.ds(0, experts - 1)], R + ch)

    def home(ch):
        for h in range(2):
            sent(X + 2 * ch + h)
            start = ch * lanes + h * half_lanes
            moved = dot(qt[...], rb[ch, h * he:(h + 1) * he].reshape(half_rows, blk)).astype(BF16)
            xs[ch, h] = moved.reshape(dp, half_lanes, blk)
            loop(1, dp, lambda i: send(
                xs.at[ch, h, dp_at(i)], g.at[d, pl.ds(start, half_lanes), :], T + ch, (e, dp_at(i))))
            g[d, start:start + half_lanes, :] = xs[ch, h, d]
        later(xr.at[ch, :, pl.ds(0, dp - 1)], T + ch)

    def score_rows():
        slot, scale = it16[:, 1:2], it16[:, 2:3]
        pick = jnp.where(iota((msg, rows), 1).astype(F32) == slot, 1.0, 0.0).astype(BF16)
        picked = dot(pick, rb[0].reshape(rows, blk))
        layer = (t16[...] + scale * picked).astype(BF16).astype(F32)
        fs[c, s_me, f_me, z] = (layer * fg_ref[:, columns(d)]).astype(BF16)
        mine = fs.at[c, s_me, f_me, z]
        loop(1, NZ, lambda i: send(mine, mine, FZ, (y * NZ + lax.rem(z + i, NZ), d)))
        later(fs.at[0, 0, 0, pl.ds(0, NZ - 1)], FZ)
        squares = jnp.sum(layer * layer, axis=-1, keepdims=True)
        sq[d] = jnp.broadcast_to(squares, (msg, 128))
        loop(1, dp, lambda i: send(sq.at[d], sq.at[d], SQ, (e, dp_at(i))))
        later(sq.at[pl.ds(0, dp - 1)], SQ)

    def score_info():
        landed(sq.at[pl.ds(0, dp - 1)], SQ)
        squares = sq[0]
        for k in range(1, dp):
            squares = squares + sq[k]
        info[y, z] = jnp.where(lane == 1, squares, it16[...])
        loop(1, NZ, lambda i: send(info.at[y, z], info.at[y, z], IZ, (y * NZ + lax.rem(z + i, NZ), d)))
        later(info.at[0, pl.ds(0, NZ - 1)], IZ)

    def to_y(i):
        return (lax.rem(y + i, NY) * NZ + z, d)

    def to_first(i):
        return (lax.rem(y + i * c, NY) * NZ + z, 2 * lax.rem(x + i * (1 - c), NX) + c)

    def to_second(i):
        return (lax.rem(y + i * (1 - c), NY) * NZ + z, 2 * lax.rem(x + i * c, NX) + c)

    def score_first():
        piece = fs.at[c, s_me, f_me]
        landed(fs.at[c, s_me, f_me, pl.ds(0, NZ - 1)], FZ)
        loop(1, NX, lambda i: send(piece, piece, FX, to_first(i)))
        loop(1, NX, lambda i: send(piece, piece, FYA, to_second(i)))
        later(fs.at[0, 0, pl.ds(0, NX - 1)], FX)
        later(fs.at[0, pl.ds(0, NX - 1), 0], FYA)

    def score_info_y():
        landed(info.at[y, pl.ds(0, NZ - 1)], IZ)
        loop(1, NY, lambda i: send(info.at[y], info.at[y], IY, to_y(i)))
        later(info.at[pl.ds(0, NY - 1)], IY)

    def score_second():
        landed(fs.at[c, s_me, pl.ds(0, NX - 1)], FX)

        def body(j):
            piece = fs.at[c, s_me, lax.rem(f_me + j, NX)]
            loop(1, NX, lambda i: send(piece, piece, FYB, to_second(i)))
        loop(1, NX, body)
        send(fs.at[c, s_me], fs.at[c, s_me], FC1, (e, sib))
        later(fs.at[0, pl.ds(0, NX - 1), pl.ds(0, NX - 1)], FYB)
        later(fs.at[0, 0], FC1)

    def score_core():
        landed(fs.at[c, pl.ds(0, NX - 1), 0], FYA)
        landed(fs.at[c, pl.ds(0, NX - 1), pl.ds(0, NX - 1)], FYB)

        def body(i):
            piece = fs.at[c, lax.rem(s_me + i, NX)]
            send(piece, piece, FC2, (e, sib))
        loop(1, NX, body)
        later(fs.at[0, pl.ds(0, NX - 1)], FC2)

    def logits_half(p):
        def term(i, values, core):
            acc[...] += lax.dot_general(
                un[:, columns(2 * i + core)], values.reshape(rows, blk), (((1,), (1,)), ((), ())),
                preferred_element_type=F32)

        @pl.when(p == 0)
        def _():
            loop(0, NX, lambda i: term(i, fs[0, :, i], 0))

        @pl.when(p == 1)
        def _():
            loop(0, NX, lambda i: term(i, fs[1, i], 1))

    def combine(ref, n):
        top = ref[0, 0:1]
        for k in range(1, n):
            top = jnp.maximum(top, ref[k, 0:1])
        total = jnp.zeros_like(top)
        picked = jnp.zeros_like(top)
        for k in range(n):
            total = total + ref[k, 1:2] * jnp.exp(ref[k, 0:1] - top)
            picked = picked + ref[k, 2:3]
        return top, total, picked

    def put(ref, at, stats):
        r8 = iota(ref.shape[1:], 0)
        ref[at] = jnp.where(r8 == 0, stats[0], jnp.where(r8 == 1, stats[1], jnp.where(r8 == 2, stats[2], 0.0)))

    def score_logits():
        acc[...] = jnp.zeros_like(acc)
        logits_half(c)
        landed(fs.at[c, 0], FC1)
        landed(fs.at[c, pl.ds(0, NX - 1)], FC2)
        logits_half(1 - c)
        landed(info.at[pl.ds(0, NY - 1)], IY)
        known = info[...].reshape(rows, 128).T
        target, squares = known[0:1], known[1:2]
        logits = acc[...] * lax.rsqrt(squares * (1.0 / width) + EPSILON)
        top = jnp.max(logits, axis=0, keepdims=True)
        total = jnp.sum(jnp.exp(logits - top), axis=0, keepdims=True)
        entry = iota(logits.shape, 0) + (e * dp + d) * logits.shape[0]
        picked = jnp.sum(jnp.where(entry.astype(F32) == target, logits, 0.0), axis=0, keepdims=True)
        put(stz, z, (top, total, picked))
        loop(1, NZ, lambda i: send(stz.at[z], stz.at[z], STZ, (y * NZ + lax.rem(z + i, NZ), d)))
        later(stz.at[pl.ds(0, NZ - 1)], STZ)

    def score_stats_y():
        landed(stz.at[pl.ds(0, NZ - 1)], STZ)
        put(sty, y, combine(stz, NZ))
        loop(1, NY, lambda i: send(sty.at[y], sty.at[y], STY, to_y(i)))
        later(sty.at[pl.ds(0, NY - 1)], STY)

    def score_stats_dp():
        landed(sty.at[pl.ds(0, NY - 1)], STY)
        put(std, d, combine(sty, NY))
        loop(1, dp, lambda i: send(std.at[d], std.at[d], STD, (e, dp_at(i))))
        later(std.at[pl.ds(0, dp - 1)], STD)

    def score_end():
        landed(std.at[pl.ds(0, dp - 1)], STD)
        top, total, picked = combine(std, dp)
        lp_ref[...] = picked - (top + jnp.log(total))

    def finish():
        for ch in range(CHUNKS):
            landed(g.at[pl.ds(0, dp - 1), pl.ds(0, lanes), :], T + ch)

        def body(k):
            at = columns(k)
            picked = dot(um[...], g[k])
            tok[:, at] = (tok[:, at].astype(F32) + rg_ref[...] * picked).astype(BF16)
            pltpu.make_async_copy(tok.at[:, at], out_h.at[:, at], osem).start()
        loop(0, dp, body)

    def expert(ch):
        gate_up(ch)
        for u in range(2):
            activate(ch, u)
        for u in range(2):
            share(ch, u)
        down(ch)

    expert(0)
    expert(1)
    gate_up(2)
    back(0)
    score_rows()
    home(0)
    score_info()
    score_first()
    activate(2, 0)
    activate(2, 1)
    score_info_y()
    score_second()
    share(2, 0)
    share(2, 1)
    down(2)
    back(1)
    home(1)
    score_core()
    back(2)
    home(2)
    score_logits()
    score_stats_y()
    finish()
    score_stats_dp()
    score_end()
    pltpu.make_async_copy(tok, out_h, osem).wait()

    for idx in list(pending):
        sent(idx)


def local(
    tokens, norm_gain, routing, route_gate, gate_weight, up_weight, down_weight,
    final_gain, unembed, targets,
):
    rows_tok, width = tokens.shape
    dp, experts = 2 * NX, NY * NZ
    blk, units, vocab = width // dp, up_weight.shape[2], unembed.shape[0]
    lanes, msg = experts * SLOTS, dp * SLOTS
    rows = experts * msg
    own = rows // dp
    vmem = pl.BlockSpec(memory_space=pltpu.VMEM)
    hbm = pl.BlockSpec(memory_space=pl.ANY)
    smem = pl.BlockSpec(memory_space=pltpu.SMEM)
    layer_out, log_probs = pl.pallas_call(
        kernel,
        out_shape=(
            jax.ShapeDtypeStruct((rows_tok, width), BF16),
            jax.ShapeDtypeStruct((1, rows), F32),
        ),
        in_specs=[hbm, vmem, vmem, vmem, smem, hbm, hbm, hbm, vmem, hbm],
        out_specs=(hbm, vmem),
        scratch_shapes=[
            pltpu.VMEM((rows_tok, 1), F32),
            pltpu.VMEM((rows_tok, width), BF16),
            pltpu.VMEM((rows_tok, width), BF16),
            pltpu.VMEM((2, blk, units), BF16),
            pltpu.VMEM((units, blk), BF16),
            pltpu.VMEM((vocab, width), BF16),
            pltpu.VMEM((CHUNKS * lanes, rows_tok), BF16),
            pltpu.VMEM((rows_tok, CHUNKS * lanes), BF16),
            pltpu.VMEM((rows // 2, rows // 2), BF16),
            pltpu.VMEM((rows // 2, rows // 2), BF16),
            pltpu.VMEM((CHUNKS, 2, dp, lanes // 2, blk), BF16),
            pltpu.VMEM((CHUNKS, 2, dp, lanes // 2, blk), BF16),
            pltpu.VMEM((CHUNKS, experts, msg, blk), BF16),
            pltpu.VMEM((CHUNKS, experts, msg, blk), BF16),
            pltpu.VMEM((CHUNKS, 2, 2, rows // 2, units), BF16),
            pltpu.VMEM((CHUNKS, 2, rows // 2, units), BF16),
            pltpu.VMEM((CHUNKS, 2, NX - 1, own, units), BF16),
            pltpu.VMEM((CHUNKS, 2, 2, NX, own, units // 2), BF16),
            pltpu.VMEM((CHUNKS, experts, msg, blk), BF16),
            pltpu.VMEM((dp, CHUNKS * lanes, blk), BF16),
            pltpu.VMEM((dp, msg, blk), BF16),
            pltpu.VMEM((dp, msg, blk), BF16),
            pltpu.VMEM((msg, blk), F32),
            pltpu.VMEM((msg, 128), F32),
            pltpu.VMEM((msg, 128), F32),
            pltpu.VMEM((dp, msg, 128), F32),
            pltpu.VMEM((NY, NZ, msg, 128), F32),
            pltpu.VMEM((dp, msg, 128), F32),
            pltpu.VMEM((2, NY, NX, NZ, msg, blk), BF16),
            pltpu.VMEM((vocab, rows), F32),
            pltpu.VMEM((8, rows), F32),
            pltpu.VMEM((NZ, 8, rows), F32),
            pltpu.VMEM((NY, 8, rows), F32),
            pltpu.VMEM((dp, 8, rows), F32),
            pltpu.SemaphoreType.DMA((SEMS,)),
            pltpu.SemaphoreType.DMA((SEMS,)),
            pltpu.SemaphoreType.DMA((7,)),
            pltpu.SemaphoreType.DMA,
        ],
        compiler_params=pltpu.CompilerParams(
            collective_id=0, has_side_effects=True, vmem_limit_bytes=VMEM_LIMIT
        ),
        name="routed_layer",
    )(
        tokens, norm_gain.reshape(1, width), routing.reshape(1, rows_tok),
        route_gate.reshape(1, rows_tok), targets, gate_weight, up_weight, down_weight,
        final_gain.reshape(1, width), unembed,
    )
    return layer_out, log_probs.reshape(rows)


def solution(mesh):
    placed = (
        P(("expert", "dp"), None),
        P(),
        P(("expert", "dp"), None),
        P(("expert", "dp")),
        P("expert", "dp", None),
        P("expert", "dp", None),
        P("expert", None, "dp"),
        P(),
        P(("expert", "dp"), None),
        P(("expert", "dp")),
    )
    return jax.shard_map(
        local,
        mesh=mesh,
        in_specs=placed,
        out_specs=(P(("expert", "dp"), None), P()),
        check_vma=False,
    )
```

time: 222 us -> 195 us (0.88)
  Pallas kernels: 215 us -> 191 us
  local copies, waits for them, and re-layouts: 6.19 us -> 3.43 us
    pallas_call x1, Pallas kernels: 215 us -> 191 us  [local(): pl.pallas_call(kernel, out_shape=(jax.ShapeDtypeStruct((rows_tok, width),...]
    unnamed x5 -> x4, local copies, waits for them, and re-layouts: 4.82 us -> 3.43 us
where the time goes in v2:
time: 195 us
  Pallas kernels  191 us (98%)
  local copies, waits for them, and re-layouts  3.43 us (2%)
    pallas_call x1, Pallas kernels, local(): pl.pallas_call(kernel, out_shape=(jax.ShapeDtypeStruct((rows_tok, width),...  191 us

profile of v2, /device:TPU:1, one launch (start us, length us, event | category | flops | bytes accessed | tf_op | source)
XLA Modules:
  0.0 195.0 jit_solution(13711374487288252768)
XLA Ops:
  0.6 190.9 %routed_layer.1 = (bf16[128,7168]{1,0:T(8,128)(2,1)}, f32[1,512]{1,0:T(1,128)}) custom-call(bf16[128,7168]{1,0:T(8,128)(2,1)} %tok_h.1, f32[1,7168]{1,0:T(1,128)} %bitcast.5, s32[1,128]{1,0:T(1,128)} %bitcast.8, f32[1,128]{1,0:T(1,128)} %bitcast.9, s32[2]{0:T(128)} %tg_ref.1, bf16[1,896,1024]{2,1,0:T(8,128)(2,1)} %wg_h.1, bf16[1,896,1024]{2,1,0:T(8,128)(2,1)} %wu_h.1, ...), custom_call_target="tpu_custom_call" | custom-call | tf_op jit(solution)/shard_map/routed_layer/pallas_call | solution.py:520
  191.6 0.0 copy-start
  191.6 2.8 %copy.14 = bf16[128,7168]{1,0:T(8,128)(2,1)} copy(bf16[128,7168]{1,0:T(8,128)(2,1)} %get-tuple-element.8) | data formatting | bytes 3670016
  194.4 0.0 copy-done
  194.4 0.6 copy.15
Async XLA Ops:
  191.6 2.9 %copy-start = (f32[1,512]{1,0:T(1,128)S(1)}, f32[1,512]{1,0:T(1,128)}, u32[]{:S(2)}) copy-start(f32[1,512]{1,0:T(1,128)} %get-tuple-element.5) | copy-start | bytes 6148

commit v3 on v2

--- a/solution.py
+++ b/solution.py
@@ -16,8 +16,9 @@
 
 X, CP, XP, HX, HC = (6 * i for i in range(5))
 Z, R, T = 30, 33, 36
-TS, IN, FZ, SQ, IZ, IY, FX, FYA, FYB, FC1, FC2, STZ, STY, STD = range(39, 53)
-SEMS = 53
+TS, IN, FZ, SQ, IZ, IY, FX, FC1, STZ, STY, STD = range(39, 50)
+FY, FC = 49, 52
+SEMS = 56
 
 F32, BF16 = jnp.float32, jnp.bfloat16
 
@@ -52,8 +53,6 @@
     own = rows // dp
     units = wd.shape[0]
     hu = units // 2
-    zh = NZ // 2
-    place_me = lax.rem(z, 2) * he + y * zh + lax.div(z, 2)
     f_me, s_me = x * (1 - c) + y * c, y * (1 - c) + x * c
 
     def send(src, dst, idx, to):
@@ -126,15 +125,9 @@
     rank_row = jnp.sum(jnp.where(same & (before < after), 1.0, 0.0), axis=0, keepdims=True)
     rank_col = jnp.sum(jnp.where(same & (after < before), 1.0, 0.0), axis=1, keepdims=True)
 
-    def place_of(expert):
-        at_y = jnp.floor(expert * (1.0 / NZ))
-        at_z = expert - at_y * NZ
-        half_z = jnp.floor(at_z * 0.5)
-        return (at_z - 2.0 * half_z) * he + at_y * zh + half_z
-
     def slot_of(rank, expert):
         chunk = jnp.floor(rank * (1.0 / SLOTS))
-        return chunk * lanes + place_of(expert) * SLOTS + (rank - chunk * SLOTS)
+        return chunk * lanes + expert * SLOTS + (rank - chunk * SLOTS)
 
     pm[...] = jnp.where(iota(pm.shape, 0).astype(F32) == slot_of(rank_row, er), 1.0, 0.0).astype(BF16)
     um[...] = jnp.where(iota(um.shape, 1).astype(F32) == slot_of(rank_col, ec), 1.0, 0.0).astype(BF16)
@@ -142,7 +135,7 @@
     lane = iota((msg, 128), 1)
     row = iota((msg, 128), 0)
     base = jnp.where(
-        lane == 1, place_of(ec[:msg]) * msg + (d * SLOTS).astype(F32) + rank_col[:msg],
+        lane == 1, ec[:msg] * msg + (d * SLOTS).astype(F32) + rank_col[:msg],
         jnp.where(lane == 2, rg_ref[0:msg, :], 0.0),
     )
     first = jnp.where(lane == 0, tg_ref[0].astype(F32), base[0:1])
@@ -162,11 +155,10 @@
     loop(0, rows_tok // tile, norm)
 
     def place(ch):
-        def body(k):
-            values = dot(pm[ch * lanes:(ch + 1) * lanes, :], nb[:, columns(k)]).astype(BF16)
+        for k in range(dp):
+            values = dot(pm[ch * lanes:(ch + 1) * lanes, :], nb[:, k * blk:(k + 1) * blk]).astype(BF16)
             xs[ch, 0, k] = values[:half_lanes]
             xs[ch, 1, k] = values[half_lanes:]
-        loop(0, dp, body)
 
     def place_send(ch):
         for h in range(2):
@@ -190,20 +182,29 @@
         top = tok[0:msg, columns(k)].astype(F32)
         ts[k] = jnp.where(r16 == 2 * d, top[0:1], jnp.where(r16 == 2 * d + 1, top[1:2], 0.0)).astype(BF16)
 
+    def spread(ch, h, into, idx):
+        elsewhere = lax.rem(lax.div(y, NY // 2) + h, 2)
+
+        def body(i):
+            to_y = h * (NY // 2) + lax.rem(y + lax.rem(i, NY // 2), NY // 2)
+            to = to_y * NZ + lax.rem(z + lax.div(i, NY // 2), NZ)
+            send(zs.at[ch, to], into.at[ch, e], idx, (to, d))
+        loop(1 - elsewhere, he, body)
+
     def dispatch(ch):
         for h in range(2):
             landed(xr.at[ch, h, pl.ds(0, dp - 1)], X + 2 * ch + h)
             moved = dot(q[...], xr[ch, h].reshape(half_rows, blk)).astype(BF16)
             zs[ch, h * he:(h + 1) * he] = moved.reshape(he, msg, blk)
-            shift = lax.rem(z + h, 2)
-
-            def body(i):
-                to_y, to_z = lax.rem(y + lax.rem(i, NY), NY), lax.rem(z + 2 * lax.div(i, NY) + shift, NZ)
-                at = h * he + to_y * zh + lax.div(to_z, 2)
-                send(zs.at[ch, at], za.at[ch, e], Z + ch, (to_y * NZ + to_z, d))
-            loop(1 - shift, he, body)
+            if ch == 0 or (ch == 2 and h == 0):
+                spread(ch, h, za, Z + ch)
+        if ch == 1:
+            loop(1, experts, lambda i: send(zs.at[ch, expert_at(i)], za.at[ch, e], Z + ch, (expert_at(i), d)))
         later(za.at[ch, pl.ds(0, experts - 1)], Z + ch)
-        za[ch, e] = zs[ch, place_me]
+        za[ch, e] = zs[ch, e]
+
+    def dispatch_rest():
+        spread(2, 1, za, Z + 2)
 
     place(0)
     permutations()
@@ -236,14 +237,10 @@
 
     def gate_up(ch):
         landed(za.at[ch, pl.ds(0, experts - 1)], Z + ch)
-        step = min(256, hu)
 
         def half(p, u):
-            def body(n):
-                at = pl.ds(pl.multiple_of(n * step, step), step)
-                values = za[ch, pl.ds(p * he, he)].reshape(he * msg, blk)
-                part[ch, u, p, :, at] = dot(values, w[u, :, at]).astype(BF16)
-            loop(0, 2 * hu // step, body)
+            values = za[ch, pl.ds(p * he, he)].reshape(he * msg, blk)
+            part[ch, u, p] = dot(values, w[u]).astype(BF16)
 
         for u in range(2):
             half(1 - c, u)
@@ -304,10 +301,10 @@
 
                 @pl.when(to != e)
                 def _():
-                    send(zs.at[ch, to], rb.at[ch, place_me], R + ch, (to, d))
+                    send(zs.at[ch, to], rb.at[ch, e], R + ch, (to, d))
             loop(0, he, give)
         loop(0, 2, body)
-        rb[ch, place_me] = zs[ch, e]
+        rb[ch, e] = zs[ch, e]
         later(rb.at[ch, pl.ds(0, experts - 1)], R + ch)
 
     def back(ch):
@@ -360,9 +357,9 @@
         piece = fs.at[c, s_me, f_me]
         landed(fs.at[c, s_me, f_me, pl.ds(0, NZ - 1)], FZ)
         loop(1, NX, lambda i: send(piece, piece, FX, to_first(i)))
-        loop(1, NX, lambda i: send(piece, piece, FYA, to_second(i)))
+        for i in (1, 3, 2):
+            send(piece, piece, FY + i, to_second(i))
         later(fs.at[0, 0, pl.ds(0, NX - 1)], FX)
-        later(fs.at[0, pl.ds(0, NX - 1), 0], FYA)
 
     def score_info_y():
         landed(info.at[y, pl.ds(0, NZ - 1)], IZ)
@@ -372,23 +369,21 @@
     def score_second():
         landed(fs.at[c, s_me, pl.ds(0, NX - 1)], FX)
 
-        def body(j):
-            piece = fs.at[c, s_me, lax.rem(f_me + j, NX)]
-            loop(1, NX, lambda i: send(piece, piece, FYB, to_second(i)))
-        loop(1, NX, body)
+        for i in (1, 3, 2):
+            def body(j):
+                piece = fs.at[c, s_me, lax.rem(f_me + j, NX)]
+                send(piece, piece, FY + i, to_second(i))
+            loop(1, NX, body)
+            later(fs.at[0, 0], FY + i)
         send(fs.at[c, s_me], fs.at[c, s_me], FC1, (e, sib))
-        later(fs.at[0, pl.ds(0, NX - 1), pl.ds(0, NX - 1)], FYB)
         later(fs.at[0, 0], FC1)
 
     def score_core():
-        landed(fs.at[c, pl.ds(0, NX - 1), 0], FYA)
-        landed(fs.at[c, pl.ds(0, NX - 1), pl.ds(0, NX - 1)], FYB)
-
-        def body(i):
-            piece = fs.at[c, lax.rem(s_me + i, NX)]
-            send(piece, piece, FC2, (e, sib))
-        loop(1, NX, body)
-        later(fs.at[0, pl.ds(0, NX - 1)], FC2)
+        for i in (1, 3, 2):
+            piece = fs.at[c, lax.rem(s_me + NX - i, NX)]
+            landed(piece, FY + i)
+            send(piece, piece, FC + i, (e, sib))
+            later(fs.at[0, 0], FC + i)
 
     def logits_half(p):
         def term(i, values, core):
@@ -419,11 +414,14 @@
         r8 = iota(ref.shape[1:], 0)
         ref[at] = jnp.where(r8 == 0, stats[0], jnp.where(r8 == 1, stats[1], jnp.where(r8 == 2, stats[2], 0.0)))
 
-    def score_logits():
+    def score_own():
         acc[...] = jnp.zeros_like(acc)
         logits_half(c)
+
+    def score_logits():
         landed(fs.at[c, 0], FC1)
-        landed(fs.at[c, pl.ds(0, NX - 1)], FC2)
+        for i in range(1, NX):
+            landed(fs.at[c, 0], FC + i)
         logits_half(1 - c)
         landed(info.at[pl.ds(0, NY - 1)], IY)
         known = info[...].reshape(rows, 128).T
@@ -474,28 +472,35 @@
         down(ch)
 
     expert(0)
-    expert(1)
-    gate_up(2)
+    dispatch_rest()
+    gate_up(1)
+    activate(1,0)
+    activate(1,1)
+    share(1,0)
+    share(1,1)
     back(0)
     score_rows()
+    score_info()
     home(0)
-    score_info()
+    gate_up(2)
+    down(1)
     score_first()
-    activate(2, 0)
-    activate(2, 1)
+    activate(2,0)
+    activate(2,1)
     score_info_y()
     score_second()
-    share(2, 0)
-    share(2, 1)
+    share(2,0)
+    share(2,1)
     down(2)
     back(1)
     home(1)
     score_core()
     back(2)
     home(2)
+    score_own()
     score_logits()
+    finish()
     score_stats_y()
-    finish()
     score_stats_dp()
     score_end()
     pltpu.make_async_copy(tok, out_h, osem).wait()

time: 195 us -> 191 us (0.979)
  Pallas kernels: 191 us -> 187 us
    pallas_call x1, Pallas kernels: 191 us -> 187 us  [local(): pl.pallas_call(kernel, out_shape=(jax.ShapeDtypeStruct((rows_tok, width),...]
where the time goes in v3:
time: 191 us
  Pallas kernels  187 us (98%)
  local copies, waits for them, and re-layouts  3.43 us (2%)
    pallas_call x1, Pallas kernels, local(): pl.pallas_call(kernel, out_shape=(jax.ShapeDtypeStruct((rows_tok, width),...  187 us

profile of v3, /device:TPU:1, one launch (start us, length us, event | category | flops | bytes accessed | tf_op | source)
XLA Modules:
  0.0 191.1 jit_solution(3135256396534302123)
XLA Ops:
  0.6 187.0 %routed_layer.1 = (bf16[128,7168]{1,0:T(8,128)(2,1)}, f32[1,512]{1,0:T(1,128)}) custom-call(bf16[128,7168]{1,0:T(8,128)(2,1)} %tok_h.1, f32[1,7168]{1,0:T(1,128)} %bitcast.5, s32[1,128]{1,0:T(1,128)} %bitcast.8, f32[1,128]{1,0:T(1,128)} %bitcast.9, s32[2]{0:T(128)} %tg_ref.1, bf16[1,896,1024]{2,1,0:T(8,128)(2,1)} %wg_h.1, bf16[1,896,1024]{2,1,0:T(8,128)(2,1)} %wu_h.1, ...), custom_call_target="tpu_custom_call" | custom-call | tf_op jit(solution)/shard_map/routed_layer/pallas_call | solution.py:525
  187.6 0.0 copy-start
  187.6 2.8 %copy.14 = bf16[128,7168]{1,0:T(8,128)(2,1)} copy(bf16[128,7168]{1,0:T(8,128)(2,1)} %get-tuple-element.8) | data formatting | bytes 3670016
  190.5 0.0 copy-done
  190.5 0.6 copy.15
Async XLA Ops:
  187.6 2.9 %copy-start = (f32[1,512]{1,0:T(1,128)S(1)}, f32[1,512]{1,0:T(1,128)}, u32[]{:S(2)}) copy-start(f32[1,512]{1,0:T(1,128)} %get-tuple-element.5) | copy-start | bytes 6148
